TPU v7x, 512 devices: a whole 4x4x16 slice. The times are simulated.
512 devices in a mesh: tile: 32 (over x, z_hi, core), dir: 16 (over y, z_lo).
Axes of the slice: x: 4, y: 4, z: 16 (z_hi: 4, z_lo: 4; z = z_hi * 4 + z_lo), core: 2. Of those that a mesh axis runs over, the one named last changes fastest.
Arguments:
- background_prev: float32 [64, 256, 128], P(None, 'tile'), may hold values from -6 to 6
- background_now: float32 [64, 256, 128], P(None, 'tile'), may hold values from -6 to 6
- stiffness: bfloat16 [64, 256, 128], P(None, 'tile'), may hold values from 0.039794922 to 0.19921875
- drift_terms: bfloat16 [3, 64, 256, 128], P(None, None, 'tile'), may hold values from -0.079589844 to 0.079589844
- born_prev: bfloat16 [64, 64, 256, 128], P('dir', None, 'tile'), may hold values from -6 to 6
- born_now: bfloat16 [64, 64, 256, 128], P('dir', None, 'tile'), may hold values from -6 to 6
- pieces: bfloat16 [64, 1024, 32, 128], P('dir', 'tile'), may hold values from -6 to 6
- piece_target: int32 [1024, 1], P('tile'), may hold values from 0 to 31; in each aligned block of 32 rows (0 to 31, 32 to 63, ...) at most 2 rows name the same one
- piece_block: int32 [1024], P('tile'), may hold values from 0 to 15
- wavelet: float32 [4], replicated, may hold values from -24 to 24
- source_cell: int32 [3], replicated, may hold values from 0 to 63
- receiver_z: int32 [256], replicated, may hold values from 0 to 63
- receiver_x: int32 [256], replicated, may hold values from 0 to 255
- receiver_y: int32 [256], replicated, may hold values from 0 to 127
Outputs:
- born_field: float32 [64, 64, 256, 128], P('dir', None, 'tile')
- traces: float32 [64, 4, 256], P('dir')
Inputs may be any that keep to these rules, and one draw needn't show every extreme that they name: `piece_target`: in each aligned block of 32 rows (the rows of one device) no tile is named by more than 2 rows; in some blocks a tile is named by exactly 2 rows.
All inputs are finite; a program needn't handle non-finite values.
Results may differ from a plain program's by a relative error of at most 0.0005.
Values may be sent and summed in bfloat16 or wider, within the bound.
No kernel may reach another device: no remote copies, remote signals or barrier semaphores. Data moves between devices by JAX's collectives and lax.ppermute only.
A program may use at most 128 MiB of HBM per device.

v0:
```python
import jax
import jax.numpy as jnp
from jax import lax
from jax.sharding import PartitionSpec as P

CX = 8
ITERS = 4
ZPARTS = 2
CAP = 2
SECOND_TAPS = (-205.0 / 72.0, 8.0 / 5.0, -1.0 / 5.0, 8.0 / 315.0, -1.0 / 560.0)
FIRST_TAPS = (0.0, 4.0 / 5.0, -1.0 / 5.0, 4.0 / 105.0, -1.0 / 280.0)


def padded_2(block, sides, width):
    for axis, dim in sides:
        count = lax.axis_size(axis)
        forward = [(i, i + 1) for i in range(count - 1)]
        backward = [(target, source) for source, target in forward]
        low = lax.ppermute(
            lax.slice_in_dim(block, block.shape[dim] - width, None, axis=dim), axis, forward
        )
        high = lax.ppermute(lax.slice_in_dim(block, 0, width, axis=dim), axis, backward)
        block = jnp.concatenate([low, block, high], axis=dim)
    return block


def shifted(padded, interior, spatial, offset):
    starts = [4, 4, 4]
    starts[spatial] = 4 + offset
    leading = padded.ndim - 3
    window = tuple(
        [slice(None)] * leading
        + [slice(starts[which], starts[which] + interior[which]) for which in range(3)]
    )
    return padded[window]


def operate(padded, stiff_wide, drift_wide):
    interior = stiff_wide.shape
    center = shifted(padded, interior, 0, 0)
    second = 3.0 * SECOND_TAPS[0] * center
    slopes = jnp.zeros_like(center)
    for spatial in range(3):
        gradient = jnp.zeros_like(center)
        for offset in range(1, 5):
            forward = shifted(padded, interior, spatial, offset)
            backward = shifted(padded, interior, spatial, -offset)
            second = second + SECOND_TAPS[offset] * (forward + backward)
            gradient = gradient + FIRST_TAPS[offset] * (forward - backward)
        slopes = slopes + drift_wide[spatial] * gradient
    return stiff_wide * second + slopes


def faces(born_present, background_part):
    return (padded_2(born_present, (("tile", 2),), 4), padded_2(background_part, (("tile", 2),), 4))


def assemble(pieces, piece_target, piece_block, tile_count):
    targets = piece_target[:, 0]
    row_count = targets.shape[0]
    positions = jnp.arange(row_count)
    before = (targets[:, None] == targets[None, :]) & (positions[None, :] < positions[:, None])
    arrival = jnp.sum(before.astype(jnp.int32), axis=1)
    slot_ids = targets * CAP + arrival
    placing = (slot_ids[:, None] == jnp.arange(tile_count * CAP)[None, :]).astype(jnp.bfloat16)
    outgoing = jnp.einsum(
        "krzy,rs->kszy", pieces, placing, preferred_element_type=jnp.float32
    ).astype(jnp.bfloat16)
    labels = jnp.dot(
        (piece_block + 1).astype(jnp.bfloat16)[None, :], placing, preferred_element_type=jnp.float32
    ).astype(jnp.bfloat16)
    incoming, arrived = (
        lax.all_to_all(outgoing, "tile", split_axis=1, concat_axis=1, tiled=True),
        lax.all_to_all(labels, "tile", split_axis=1, concat_axis=1, tiled=True),
    )
    wanted = (jnp.arange(ZPARTS * CX) + 1).astype(jnp.float32)
    picking = (
        (arrived[0][:, None].astype(jnp.float32) == wanted[None, :])
        .astype(jnp.bfloat16)
        .reshape(-1, ZPARTS, CX)
    )
    perturb = jnp.einsum("kszy,spx->kpzxy", incoming, picking, preferred_element_type=jnp.float32)
    return perturb.reshape(pieces.shape[0], ZPARTS * pieces.shape[2], CX, pieces.shape[3])


def local(
    background_prev,
    background_now,
    stiffness,
    drift_terms,
    born_prev,
    born_now,
    pieces,
    piece_target,
    piece_block,
    wavelet,
    source_cell,
    receiver_z,
    receiver_x,
    receiver_y,
):
    tile_count = lax.axis_size("tile")
    tile_place = lax.axis_index("tile")
    depth_cells, width_cells, height_cells = background_now.shape
    stiff_wide = stiffness.astype(jnp.float32)
    drift_wide = drift_terms.astype(jnp.float32)
    perturb = assemble(pieces, piece_target, piece_block, tile_count)
    across_axis = (tile_place * width_cells + jnp.arange(width_cells))[None, :, None]
    height_axis = jnp.arange(height_cells)[None, None, :]
    earlier_born = born_prev.astype(jnp.float32)
    current_born = born_now.astype(jnp.float32)
    local_x = receiver_x - tile_place * width_cells
    inside = ((local_x >= 0) & (local_x < width_cells)).astype(jnp.float32)
    flat_index = (
        receiver_z * width_cells + jnp.clip(local_x, 0, width_cells - 1)
    ) * height_cells + receiver_y
    slab_cells = depth_cells // lax.axis_size("dir")
    slab_start = lax.axis_index("dir") * slab_cells
    previous = lax.dynamic_slice_in_dim(background_prev, slab_start, slab_cells, 0)
    present = lax.dynamic_slice_in_dim(background_now, slab_start, slab_cells, 0)
    slab_stiff = lax.dynamic_slice_in_dim(stiff_wide, slab_start, slab_cells, 0)
    slab_drift = lax.dynamic_slice_in_dim(drift_wide, slab_start, slab_cells, 1)
    depth_axis = (slab_start + jnp.arange(slab_cells))[:, None, None]
    source_mask = (
        (depth_axis == source_cell[0])
        & (across_axis == source_cell[1])
        & (height_axis == source_cell[2])
    ).astype(jnp.float32)
    records = []
    for step_index in range(ITERS):
        deeper = padded_2(present[None], (("dir", 1),), 4)
        born_wide, back_wide = faces(current_born, deeper)
        local_accel = operate(
            jnp.pad(back_wide[0], ((0, 0), (0, 0), (4, 4))), slab_stiff, slab_drift
        )
        acceleration = lax.all_gather(local_accel, "dir", axis=0, tiled=True)
        previous, present = (
            present,
            2.0 * present - previous + local_accel + wavelet[step_index] * source_mask,
        )
        born_padded = jnp.pad(born_wide, ((0, 0), (4, 4), (0, 0), (4, 4)))
        following = (
            2.0 * current_born
            - earlier_born
            + operate(born_padded, stiff_wide, drift_wide)
            + perturb * acceleration
        )
        records.append(
            jnp.take(following.reshape(following.shape[0], -1), flat_index, axis=1)
            * inside[None, :]
        )
        earlier_born, current_born = (current_born, following)
    traces = lax.psum(jnp.stack(records, axis=1), "tile")
    return (current_born, traces)


def solution(mesh):
    placed = (
        P(None, "tile", None),
        P(None, "tile", None),
        P(None, "tile", None),
        P(None, None, "tile", None),
        P("dir", None, "tile", None),
        P("dir", None, "tile", None),
        P("dir", "tile", None, None),
        P("tile", None),
        P("tile"),
        P(),
        P(),
        P(),
        P(),
        P(),
    )
    return jax.shard_map(
        local,
        mesh=mesh,
        in_specs=placed,
        out_specs=(P("dir", None, "tile", None), P("dir", None, None)),
        check_vma=False,
    )
```

profile of v0, /device:TPU:24, one launch (start us, length us, event | category | flops | bytes accessed | tf_op | source)
XLA Modules:
  0.0 746.2 jit_solution(9172707135732427772)
XLA Ops:
  0.6 0.9 convert_reduce_fusion.1
  2.2 0.8 fusion.9
  3.8 17.9 %all-to-all-start = ((bf16[1,32,2]{2,0,1:T(2,128)(2,1)}), bf16[1,32,2]{2,0,1:T(2,128)(2,1)S(1)}, u32[]{:S(2)}, u32[]{:S(2)}) async-start(bf16[1,32,2]{2,0,1:T(2,128)(2,1)} %all_to_all.12), calls=%async_computation | async-start | bytes 32768 | tf_op jit(solution)/shard_map/all_to_all | solution.py:74
  21.8 0.8 convert_bitcast_fusion
  22.6 2.8 copy.42
  25.4 10.8 %all-to-all-done = bf16[1,32,2]{2,0,1:T(2,128)(2,1)S(1)} async-done(((bf16[1,32,2]{2,0,1:T(2,128)(2,1)}), bf16[1,32,2]{2,0,1:T(2,128)(2,1)S(1)}, u32[]{:S(2)}, u32[]{:S(2)}) %all-to-all-start) | async-done | bytes 160 | tf_op jit(solution)/shard_map/all_to_all | solution.py:74
  36.3 4.8 all-to-all-start.1
  41.8 4.0 collective-permute-start.3
  45.8 1.9 collective-permute-start.2
  47.7 1.1 fusion.119
  48.8 1.3 collective-permute-start.1
  50.1 3.8 collective-permute-start
  54.1 0.7 fusion.125
  56.8 0.9 slice_bitcast_fusion.2
  57.7 67.6 %collective-permute-done.3 = f32[1,4,8,128]{3,2,1,0:T(8,128)S(1)} collective-permute-done((f32[1,4,8,128]{3,2,1,0:T(8,128)S(1)}, f32[1,4,8,128]{3,2,1,0:T(8,128)S(1)}, u32[]{:S(2)}, u32[]{:S(2)}) %collective-permute-start.3) | collective-permute-done | bytes 16416 | tf_op jit(solution)/shard_map/ppermute | solution.py:22
  125.4 1.3 collective-permute-start.5
  126.7 3.0 collective-permute-start.4
  130.6 1.5 fusion.39
  132.1 27.6 %collective-permute-start.9 = (f32[1,4,8,128]{3,2,1,0:T(8,128)S(1)}, f32[1,4,8,128]{3,2,1,0:T(8,128)S(1)}, u32[]{:S(2)}, u32[]{:S(2)}) collective-permute-start(f32[1,4,8,128]{3,2,1,0:T(8,128)S(1)} %bitcast.136), channel_id=1, source_target_pairs={{1,0},{2,1},{3,2},{4,3},{5,4},{6,5},{7,6},{8,7},{9,8},{10,9},{11,1... | collective-permute-start | bytes 49160 | tf_op jit(solution)/shard_map/ppermute | solution.py:22
  159.8 1.9 collective-permute-start.8
  161.9 6.2 collective-permute-done.8
  168.1 1.3 collective-permute-start.11
  169.4 10.4 %collective-permute-start.10 = (f32[1,12,4,128]{3,2,1,0:T(4,128)S(1)}, f32[1,12,4,128]{3,2,1,0:T(4,128)S(1)}, u32[]{:S(2)}, u32[]{:S(2)}) collective-permute-start(f32[1,12,4,128]{3,2,1,0:T(4,128)S(1)} %get-tuple-element.30), channel_id=1, source_target_pairs={{0,16},{16,32},{32,48},{48,64},{64,80},{80,96},{96,112},{112,128},... | collective-permute-start | bytes 73736 | tf_op jit(solution)/shard_map/ppermute | solution.py:19
  179.8 37.0 %all_gather.12 = f32[64,8,128]{2,1,0:T(8,128)} all-gather(f32[4,8,128]{2,1,0:T(8,128)S(1)} %get-tuple-element.14), channel_id=1, replica_groups=mesh['tile'=32,'dir'=16] {'dir'}, dimensions={0}, use_global_device_ids=true | all-gather | bytes 278528 | tf_op jit(solution)/shard_map/all_gather | solution.py:136
  216.8 1.5 fusion.108
  218.3 3.6 collective-permute-start.15
  221.9 2.2 collective-permute-start.14
  224.2 5.3 select_maximum_fusion.6
  229.5 3.0 fusion.6
  232.5 7.7 %multiply_add_fusion.3 = f32[4,64,8,128]{3,2,1,0:T(8,128)S(1)} fusion(f32[4,64,8,128]{3,2,1,0:T(8,128)S(1)} %bitcast.132, f32[4,72,16,136]{3,2,1,0:T(8,128)S(1)} %copy-done.2, f32[4,64,4,128]{3,2,1,0:T(4,128)S(1)} %copy-done.15, f32[4,64,8,128]{3,2,1,0:T(8,128)S(1)} %convert_element_type.62, f32[4,64,4,128]{3,2,1,0:T(4,128)} %collective-permute-done, ...), kind=kLoop, calls=%fused_computation.110 | loop fusion | flops 23855104 | bytes 22806528 | tf_op jit(solution)/shard_map/add | solution.py:143
  240.4 1.4 collective-permute-start.7
  241.9 3.1 collective-permute-start.6
  245.0 1.3 collective-permute-start.17
  246.3 7.5 collective-permute-start.16
  253.7 49.0 %all_gather.13 = f32[64,8,128]{2,1,0:T(8,128)S(1)} all-gather(f32[4,8,128]{2,1,0:T(8,128)S(1)} %get-tuple-element.12), channel_id=1, replica_groups=mesh['tile'=32,'dir'=16] {'dir'}, dimensions={0}, use_global_device_ids=true | all-gather | bytes 278528 | tf_op jit(solution)/shard_map/all_gather | solution.py:136
  302.8 2.7 select_maximum_fusion.4
  305.5 6.1 multiply_add_fusion.2
  311.8 1.3 collective-permute-start.13
  313.1 3.1 collective-permute-start.12
  316.1 2.2 fusion.42
  318.4 3.2 collective-permute-start.21
  321.5 3.0 collective-permute-start.20
  324.5 46.2 %all_gather.14 = f32[64,8,128]{2,1,0:T(8,128)S(1)} all-gather(f32[4,8,128]{2,1,0:T(8,128)S(1)} %get-tuple-element.10), channel_id=1, replica_groups=mesh['tile'=32,'dir'=16] {'dir'}, dimensions={0}, use_global_device_ids=true | all-gather | bytes 278528 | tf_op jit(solution)/shard_map/all_gather | solution.py:136
  370.7 1.3 collective-permute-start.23
  372.0 3.2 collective-permute-start.22
  375.2 2.7 select_maximum_fusion.2
  377.9 6.1 multiply_add_fusion.1
  384.0 1.0 copy-done.3
  384.9 1.1 fusion.116
  386.1 1.3 collective-permute-start.19
  387.4 11.4 %collective-permute-start.18 = (f32[4,64,4,128]{3,2,1,0:T(4,128)}, f32[4,64,4,128]{3,2,1,0:T(4,128)}, u32[]{:S(2)}, u32[]{:S(2)}) collective-permute-start(f32[4,64,4,128]{3,2,1,0:T(4,128)} %get-tuple-element.15), channel_id=1, source_target_pairs={{0,16},{16,32},{32,48},{48,64},{64,80},{80,96},{96,112},{112,128},... | collective-permute-start | bytes 1572872 | tf_op jit(solution)/shard_map/ppermute | solution.py:19
  398.9 0.9 fusion.56
  399.7 48.9 %all_gather.15 = f32[64,8,128]{2,1,0:T(8,128)} all-gather(f32[4,8,128]{2,1,0:T(8,128)S(1)} %fusion.56), channel_id=1, replica_groups=mesh['tile'=32,'dir'=16] {'dir'}, dimensions={0}, use_global_device_ids=true | all-gather | bytes 278528 | tf_op jit(solution)/shard_map/all_gather | solution.py:136
  448.6 15.9 %copy.45 = f32[4,64,8,128]{0,3,2,1:T(8,128)} copy(f32[4,64,8,128]{3,2,1,0:T(8,128)S(1)} %multiply_add_fusion.3) | data formatting | bytes 2097152 | tf_op jit(solution)/shard_map/add | solution.py:143
  464.6 11.3 %gather_fusion = f32[256,4]{1,0:T(8,128)S(1)} fusion(f32[4,65536]{0,1:T(8,128)} %bitcast.128, s32[1024]{0:T(1024)S(1)} %pad_clamp_fusion), kind=kCustom, calls=%fused_computation.clone | custom fusion | bytes 9216 | tf_op jit(solution)/shard_map/jit(_take)/gather | solution.py:149
  475.8 16.0 %copy.46 = f32[4,64,8,128]{0,3,2,1:T(8,128)} copy(f32[4,64,8,128]{3,2,1,0:T(8,128)S(1)} %multiply_add_fusion.2) | data formatting | bytes 2097152 | tf_op jit(solution)/shard_map/add | solution.py:143
  491.8 11.9 %gather_fusion.1 = f32[256,4]{1,0:T(8,128)} fusion(f32[4,65536]{0,1:T(8,128)} %bitcast.130, s32[1024]{0:T(1024)S(1)} %pad_clamp_fusion), kind=kCustom, calls=%fused_computation.1.clone | custom fusion | bytes 9216 | tf_op jit(solution)/shard_map/jit(_take)/gather | solution.py:149
  503.7 16.0 %copy.47 = f32[4,64,8,128]{0,3,2,1:T(8,128)} copy(f32[4,64,8,128]{3,2,1,0:T(8,128)S(1)} %copy-done.4) | data formatting | bytes 2097152 | tf_op jit(solution)/shard_map/add | solution.py:143
  519.7 11.9 %gather_fusion.2 = f32[256,4]{1,0:T(8,128)} fusion(f32[4,65536]{0,1:T(8,128)} %bitcast.131, s32[1024]{0:T(1024)S(1)} %pad_clamp_fusion), kind=kCustom, calls=%fused_computation.2.clone | custom fusion | bytes 9216 | tf_op jit(solution)/shard_map/jit(_take)/gather | solution.py:149
  531.6 3.8 select_maximum_fusion
  535.4 8.5 %multiply_add_fusion = f32[4,64,8,128]{3,2,1,0:T(8,128)} fusion(f32[4,64,8,128]{3,2,1,0:T(8,128)S(1)} %bitcast.135, f32[4,72,16,136]{3,2,1,0:T(8,128)S(1)} %select_maximum_fusion, f32[4,64,4,128]{3,2,1,0:T(4,128)} %collective-permute-done.19, f32[4,64,8,128]{3,2,1,0:T(8,128)S(1)} %copy-done.4, f32[4,64,4,128]{3,2,1,0:T(4,128)} %collective-permute-done.18, ...), kind=kLoop, calls=%fused_computation.107 | loop fusion | flops 23592960 | bytes 23330816 | tf_op jit(solution)/shard_map/add | solution.py:143
  543.9 16.9 %copy.48 = f32[4,64,8,128]{0,3,2,1:T(8,128)} copy(f32[4,64,8,128]{3,2,1,0:T(8,128)} %multiply_add_fusion) | data formatting | bytes 2097152 | tf_op jit(solution)/shard_map/add | solution.py:143
  560.8 11.3 %gather_fusion.3 = f32[256,4]{1,0:T(8,128)S(1)} fusion(f32[4,65536]{0,1:T(8,128)} %bitcast.129, s32[1024]{0:T(1024)S(1)} %pad_clamp_fusion), kind=kCustom, calls=%fused_computation.3.clone | custom fusion | bytes 9216 | tf_op jit(solution)/shard_map/jit(_take)/gather | solution.py:149
  572.6 173.6 %psum.7 = f32[4,4,256]{2,1,0:T(4,128)} all-reduce(f32[4,4,256]{2,1,0:T(4,128)S(1)} %pad_maximum_fusion.12), channel_id=1, replica_groups=mesh['tile'=32,'dir'=16] {'tile'}, use_global_device_ids=true, to_apply=%region_1.3 | all-reduce | flops 4096 | bytes 32768 | tf_op jit(solution)/shard_map/psum | solution.py:153
  (111 shorter events, 6.3 us)
Async XLA Ops:
  0.6 21.2 %copy-start = (bf16[4,32,32,128]{3,2,1,0:T(8,128)(2,1)S(1)}, bf16[4,32,32,128]{3,2,1,0:T(8,128)(2,1)}, u32[]{:S(2)}) copy-start(bf16[4,32,32,128]{3,2,1,0:T(8,128)(2,1)} %param.22) | copy-start | bytes 3145732
  3.8 32.4 %all-to-all-start = ((bf16[1,32,2]{2,0,1:T(2,128)(2,1)}), bf16[1,32,2]{2,0,1:T(2,128)(2,1)S(1)}, u32[]{:S(2)}, u32[]{:S(2)}) async-start(bf16[1,32,2]{2,0,1:T(2,128)(2,1)} %all_to_all.12), calls=%async_computation | async-start | bytes 32768 | tf_op jit(solution)/shard_map/all_to_all | solution.py:74
  22.6 25.1 %copy-start.5 = (bf16[4,64,8,128]{3,2,1,0:T(8,128)(2,1)S(1)}, bf16[4,64,8,128]{3,2,1,0:T(8,128)(2,1)}, u32[]{:S(2)}) copy-start(bf16[4,64,8,128]{3,2,1,0:T(8,128)(2,1)} %param.21) | copy-start | bytes 1572868
  22.6 31.3 %copy-start.17 = (bf16[3,64,8,128]{3,2,1,0:T(8,128)(2,1)S(1)}, bf16[3,64,8,128]{3,2,1,0:T(8,128)(2,1)}, u32[]{:S(2)}) copy-start(bf16[3,64,8,128]{3,2,1,0:T(8,128)(2,1)} %param.19) | copy-start | bytes 1179652
  25.4 28.6 %copy-start.21 = (s32[3]{0:T(128)S(1)}, s32[3]{0:T(128)}, u32[]{:S(2)}) copy-start(s32[3]{0:T(128)} %param.26) | copy-start | bytes 40
  25.4 30.6 %copy-start.22 = (f32[4]{0:T(128)S(1)}, f32[4]{0:T(128)}, u32[]{:S(2)}) copy-start(f32[4]{0:T(128)} %param.25) | copy-start | bytes 52
  25.4 31.4 %copy-start.23 = (s32[256]{0:T(256)S(1)}, s32[256]{0:T(256)}, u32[]{:S(2)}) copy-start(s32[256]{0:T(256)} %param.29) | copy-start | bytes 3076
  25.4 31.4 %copy-start.24 = (s32[256]{0:T(256)S(1)}, s32[256]{0:T(256)}, u32[]{:S(2)}) copy-start(s32[256]{0:T(256)} %param.28) | copy-start | bytes 3076
  25.4 31.4 %copy-start.25 = (s32[256]{0:T(256)S(1)}, s32[256]{0:T(256)}, u32[]{:S(2)}) copy-start(s32[256]{0:T(256)} %param.27) | copy-start | bytes 3076
  25.4 105.0 %copy-start.20 = (bf16[64,8,128]{2,1,0:T(8,128)(2,1)S(1)}, bf16[64,8,128]{2,1,0:T(8,128)(2,1)}, u32[]{:S(2)}) copy-start(bf16[64,8,128]{2,1,0:T(8,128)(2,1)} %param.18) | copy-start | bytes 393220
  36.3 193.2 %all-to-all-start.1 = ((bf16[4,64,32,128]{3,2,0,1:T(8,128)(2,1)}), bf16[4,64,32,128]{3,2,0,1:T(8,128)(2,1)}, u32[]{:S(2)}, u32[]{:S(2)}) async-start(bf16[4,64,32,128]{3,2,0,1:T(8,128)(2,1)} %copy.42), calls=%async_computation.1 | async-start | bytes 4194304 | tf_op jit(solution)/shard_map/all_to_all | solution.py:73
  41.8 83.6 %collective-permute-start.3 = (f32[1,4,8,128]{3,2,1,0:T(8,128)S(1)}, f32[1,4,8,128]{3,2,1,0:T(8,128)S(1)}, u32[]{:S(2)}, u32[]{:S(2)}) collective-permute-start(f32[1,4,8,128]{3,2,1,0:T(8,128)S(1)} %dynamic-slice_bitcast_fusion.3), channel_id=1, source_target_pairs={{1,0},{2,1},{3,2},{4,3},{5,4},{6,5},{7,6},{8,7},{9,8},{10,9},{11,1... | collective-permute-start | bytes 49160 | tf_op jit(solution)/shard_map/ppermute | solution.py:22
  45.8 79.6 %collective-permute-start.2 = (f32[1,4,8,128]{3,2,1,0:T(8,128)S(1)}, f32[1,4,8,128]{3,2,1,0:T(8,128)S(1)}, u32[]{:S(2)}, u32[]{:S(2)}) collective-permute-start(f32[1,4,8,128]{3,2,1,0:T(8,128)S(1)} %dynamic-slice_bitcast_fusion.3), channel_id=1, source_target_pairs={{0,1},{1,2},{2,3},{3,4},{4,5},{5,6},{6,7},{7,8},{8,9},{9,10},{10,1... | collective-permute-start | bytes 49160 | tf_op jit(solution)/shard_map/ppermute | solution.py:19
  48.8 175.3 %collective-permute-start.1 = (f32[4,64,4,128]{3,2,1,0:T(4,128)}, f32[4,64,4,128]{3,2,1,0:T(4,128)S(1)}, u32[]{:S(2)}, u32[]{:S(2)}) collective-permute-start(f32[4,64,4,128]{3,2,1,0:T(4,128)} %get-tuple-element.25), channel_id=1, source_target_pairs={{16,0},{32,16},{48,32},{64,48},{80,64},{96,80},{112,96},{128,112},... | collective-permute-start | bytes 1572872 | tf_op jit(solution)/shard_map/ppermute | solution.py:22
  50.1 174.0 %collective-permute-start = (f32[4,64,4,128]{3,2,1,0:T(4,128)}, f32[4,64,4,128]{3,2,1,0:T(4,128)}, u32[]{:S(2)}, u32[]{:S(2)}) collective-permute-start(f32[4,64,4,128]{3,2,1,0:T(4,128)} %get-tuple-element.24), channel_id=1, source_target_pairs={{0,16},{16,32},{32,48},{48,64},{64,80},{80,96},{96,112},{112,128},... | collective-permute-start | bytes 1572872 | tf_op jit(solution)/shard_map/ppermute | solution.py:19
  54.0 175.4 %copy-start.13 = (f32[3,64,8,128]{3,2,1,0:T(8,128)}, f32[3,64,8,128]{3,2,1,0:T(8,128)S(1)}, u32[]{:S(2)}) copy-start(f32[3,64,8,128]{3,2,1,0:T(8,128)S(1)} %convert_element_type.65) | copy-start | bytes 2359300
  125.4 5.1 collective-permute-start.5
  126.7 3.9 collective-permute-start.4
  132.1 29.7 %collective-permute-start.9 = (f32[1,4,8,128]{3,2,1,0:T(8,128)S(1)}, f32[1,4,8,128]{3,2,1,0:T(8,128)S(1)}, u32[]{:S(2)}, u32[]{:S(2)}) collective-permute-start(f32[1,4,8,128]{3,2,1,0:T(8,128)S(1)} %bitcast.136), channel_id=1, source_target_pairs={{1,0},{2,1},{3,2},{4,3},{5,4},{6,5},{7,6},{8,7},{9,8},{10,9},{11,1... | collective-permute-start | bytes 49160 | tf_op jit(solution)/shard_map/ppermute | solution.py:22
  159.8 8.3 %collective-permute-start.8 = (f32[1,4,8,128]{3,2,1,0:T(8,128)S(1)}, f32[1,4,8,128]{3,2,1,0:T(8,128)S(1)}, u32[]{:S(2)}, u32[]{:S(2)}) collective-permute-start(f32[1,4,8,128]{3,2,1,0:T(8,128)S(1)} %bitcast.137), channel_id=1, source_target_pairs={{0,1},{1,2},{2,3},{3,4},{4,5},{5,6},{6,7},{7,8},{8,9},{9,10},{10,1... | collective-permute-start | bytes 49160 | tf_op jit(solution)/shard_map/ppermute | solution.py:19
  168.1 48.6 %collective-permute-start.11 = (f32[1,12,4,128]{3,2,1,0:T(4,128)S(1)}, f32[1,12,4,128]{3,2,1,0:T(4,128)S(1)}, u32[]{:S(2)}, u32[]{:S(2)}) collective-permute-start(f32[1,12,4,128]{3,2,1,0:T(4,128)S(1)} %get-tuple-element.31), channel_id=1, source_target_pairs={{16,0},{32,16},{48,32},{64,48},{80,64},{96,80},{112,96},{128,112},... | collective-permute-start | bytes 73736 | tf_op jit(solution)/shard_map/ppermute | solution.py:22
  169.4 47.3 %collective-permute-start.10 = (f32[1,12,4,128]{3,2,1,0:T(4,128)S(1)}, f32[1,12,4,128]{3,2,1,0:T(4,128)S(1)}, u32[]{:S(2)}, u32[]{:S(2)}) collective-permute-start(f32[1,12,4,128]{3,2,1,0:T(4,128)S(1)} %get-tuple-element.30), channel_id=1, source_target_pairs={{0,16},{16,32},{32,48},{48,64},{64,80},{80,96},{96,112},{112,128},... | collective-permute-start | bytes 73736 | tf_op jit(solution)/shard_map/ppermute | solution.py:19
  218.3 26.6 %collective-permute-start.15 = (f32[1,4,8,128]{3,2,1,0:T(8,128)S(1)}, f32[1,4,8,128]{3,2,1,0:T(8,128)S(1)}, u32[]{:S(2)}, u32[]{:S(2)}) collective-permute-start(f32[1,4,8,128]{3,2,1,0:T(8,128)S(1)} %get-tuple-element.11), channel_id=1, source_target_pairs={{1,0},{2,1},{3,2},{4,3},{5,4},{6,5},{7,6},{8,7},{9,8},{10,9},{11,1... | collective-permute-start | bytes 49160 | tf_op jit(solution)/shard_map/ppermute | solution.py:22
  221.9 23.0 %collective-permute-start.14 = (f32[1,4,8,128]{3,2,1,0:T(8,128)S(1)}, f32[1,4,8,128]{3,2,1,0:T(8,128)S(1)}, u32[]{:S(2)}, u32[]{:S(2)}) collective-permute-start(f32[1,4,8,128]{3,2,1,0:T(8,128)S(1)} %get-tuple-element.11), channel_id=1, source_target_pairs={{0,1},{1,2},{2,3},{3,4},{4,5},{5,6},{6,7},{7,8},{8,9},{9,10},{10,1... | collective-permute-start | bytes 49160 | tf_op jit(solution)/shard_map/ppermute | solution.py:19
  224.2 5.3 copy-start.14
  229.5 3.1 copy-start.2
  229.5 3.1 copy-start.15
  240.2 65.2 %copy-start.6 = (bf16[4,64,8,128]{3,2,1,0:T(8,128)(2,1)S(1)}, bf16[4,64,8,128]{3,2,1,0:T(8,128)(2,1)}, u32[]{:S(2)}) copy-start(bf16[4,64,8,128]{3,2,1,0:T(8,128)(2,1)} %param.21) | copy-start | bytes 1572868
  240.2 65.2 %copy-start.7 = (f32[64,8,128]{2,1,0:T(8,128)S(1)}, f32[64,8,128]{2,1,0:T(8,128)}, u32[]{:S(2)}) copy-start(f32[64,8,128]{2,1,0:T(8,128)} %get-tuple-element.21) | copy-start | bytes 786436
  240.2 65.2 %copy-start.9 = (f32[64,8,128]{2,1,0:T(8,128)S(1)}, f32[64,8,128]{2,1,0:T(8,128)}, u32[]{:S(2)}) copy-start(f32[64,8,128]{2,1,0:T(8,128)} %get-tuple-element.22) | copy-start | bytes 786436
  240.2 65.2 %copy-start.11 = (f32[64,8,128]{2,1,0:T(8,128)S(1)}, f32[64,8,128]{2,1,0:T(8,128)}, u32[]{:S(2)}) copy-start(f32[64,8,128]{2,1,0:T(8,128)} %get-tuple-element.23) | copy-start | bytes 786436
  240.4 62.3 %collective-permute-start.7 = (f32[4,64,4,128]{3,2,1,0:T(4,128)S(1)}, f32[4,64,4,128]{3,2,1,0:T(4,128)S(1)}, u32[]{:S(2)}, u32[]{:S(2)}) collective-permute-start(f32[4,64,4,128]{3,2,1,0:T(4,128)S(1)} %get-tuple-element.20), channel_id=1, source_target_pairs={{16,0},{32,16},{48,32},{64,48},{80,64},{96,80},{112,96},{128,112},... | collective-permute-start | bytes 1572872 | tf_op jit(solution)/shard_map/ppermute | solution.py:22
  241.9 60.9 %collective-permute-start.6 = (f32[4,64,4,128]{3,2,1,0:T(4,128)S(1)}, f32[4,64,4,128]{3,2,1,0:T(4,128)S(1)}, u32[]{:S(2)}, u32[]{:S(2)}) collective-permute-start(f32[4,64,4,128]{3,2,1,0:T(4,128)S(1)} %get-tuple-element.19), channel_id=1, source_target_pairs={{0,16},{16,32},{32,48},{48,64},{64,80},{80,96},{96,112},{112,128},... | collective-permute-start | bytes 1572872 | tf_op jit(solution)/shard_map/ppermute | solution.py:19
  245.0 57.7 %collective-permute-start.17 = (f32[1,12,4,128]{3,2,1,0:T(4,128)S(1)}, f32[1,12,4,128]{3,2,1,0:T(4,128)S(1)}, u32[]{:S(2)}, u32[]{:S(2)}) collective-permute-start(f32[1,12,4,128]{3,2,1,0:T(4,128)S(1)} %get-tuple-element.29), channel_id=1, source_target_pairs={{16,0},{32,16},{48,32},{64,48},{80,64},{96,80},{112,96},{128,112},... | collective-permute-start | bytes 73736 | tf_op jit(solution)/shard_map/ppermute | solution.py:22
  246.3 56.4 %collective-permute-start.16 = (f32[1,12,4,128]{3,2,1,0:T(4,128)S(1)}, f32[1,12,4,128]{3,2,1,0:T(4,128)S(1)}, u32[]{:S(2)}, u32[]{:S(2)}) collective-permute-start(f32[1,12,4,128]{3,2,1,0:T(4,128)S(1)} %get-tuple-element.28), channel_id=1, source_target_pairs={{0,16},{16,32},{32,48},{48,64},{64,80},{80,96},{96,112},{112,128},... | collective-permute-start | bytes 73736 | tf_op jit(solution)/shard_map/ppermute | solution.py:19
  311.8 63.4 %collective-permute-start.13 = (f32[4,64,4,128]{3,2,1,0:T(4,128)S(1)}, f32[4,64,4,128]{3,2,1,0:T(4,128)S(1)}, u32[]{:S(2)}, u32[]{:S(2)}) collective-permute-start(f32[4,64,4,128]{3,2,1,0:T(4,128)S(1)} %get-tuple-element.18), channel_id=1, source_target_pairs={{16,0},{32,16},{48,32},{64,48},{80,64},{96,80},{112,96},{128,112},... | collective-permute-start | bytes 1572872 | tf_op jit(solution)/shard_map/ppermute | solution.py:22
  313.1 62.1 %collective-permute-start.12 = (f32[4,64,4,128]{3,2,1,0:T(4,128)S(1)}, f32[4,64,4,128]{3,2,1,0:T(4,128)S(1)}, u32[]{:S(2)}, u32[]{:S(2)}) collective-permute-start(f32[4,64,4,128]{3,2,1,0:T(4,128)S(1)} %get-tuple-element.17), channel_id=1, source_target_pairs={{0,16},{16,32},{32,48},{48,64},{64,80},{80,96},{96,112},{112,128},... | collective-permute-start | bytes 1572872 | tf_op jit(solution)/shard_map/ppermute | solution.py:19
  318.4 52.3 %collective-permute-start.21 = (f32[1,4,8,128]{3,2,1,0:T(8,128)S(1)}, f32[1,4,8,128]{3,2,1,0:T(8,128)S(1)}, u32[]{:S(2)}, u32[]{:S(2)}) collective-permute-start(f32[1,4,8,128]{3,2,1,0:T(8,128)S(1)} %get-tuple-element.9), channel_id=1, source_target_pairs={{1,0},{2,1},{3,2},{4,3},{5,4},{6,5},{7,6},{8,7},{9,8},{10,9},{11,1... | collective-permute-start | bytes 49160 | tf_op jit(solution)/shard_map/ppermute | solution.py:22
  321.5 49.1 %collective-permute-start.20 = (f32[1,4,8,128]{3,2,1,0:T(8,128)S(1)}, f32[1,4,8,128]{3,2,1,0:T(8,128)S(1)}, u32[]{:S(2)}, u32[]{:S(2)}) collective-permute-start(f32[1,4,8,128]{3,2,1,0:T(8,128)S(1)} %get-tuple-element.9), channel_id=1, source_target_pairs={{0,1},{1,2},{2,3},{3,4},{4,5},{5,6},{6,7},{7,8},{8,9},{9,10},{10,1... | collective-permute-start | bytes 49160 | tf_op jit(solution)/shard_map/ppermute | solution.py:19
  370.7 28.1 %collective-permute-start.23 = (f32[1,12,4,128]{3,2,1,0:T(4,128)S(1)}, f32[1,12,4,128]{3,2,1,0:T(4,128)S(1)}, u32[]{:S(2)}, u32[]{:S(2)}) collective-permute-start(f32[1,12,4,128]{3,2,1,0:T(4,128)S(1)} %get-tuple-element.27), channel_id=1, source_target_pairs={{16,0},{32,16},{48,32},{64,48},{80,64},{96,80},{112,96},{128,112},... | collective-permute-start | bytes 73736 | tf_op jit(solution)/shard_map/ppermute | solution.py:22
  372.0 26.8 %collective-permute-start.22 = (f32[1,12,4,128]{3,2,1,0:T(4,128)S(1)}, f32[1,12,4,128]{3,2,1,0:T(4,128)S(1)}, u32[]{:S(2)}, u32[]{:S(2)}) collective-permute-start(f32[1,12,4,128]{3,2,1,0:T(4,128)S(1)} %get-tuple-element.26), channel_id=1, source_target_pairs={{0,16},{16,32},{32,48},{48,64},{64,80},{80,96},{96,112},{112,128},... | collective-permute-start | bytes 73736 | tf_op jit(solution)/shard_map/ppermute | solution.py:19
  384.0 1.0 copy-start.3
  386.1 145.5 %collective-permute-start.19 = (f32[4,64,4,128]{3,2,1,0:T(4,128)}, f32[4,64,4,128]{3,2,1,0:T(4,128)}, u32[]{:S(2)}, u32[]{:S(2)}) collective-permute-start(f32[4,64,4,128]{3,2,1,0:T(4,128)} %get-tuple-element.16), channel_id=1, source_target_pairs={{16,0},{32,16},{48,32},{64,48},{80,64},{96,80},{112,96},{128,112},... | collective-permute-start | bytes 1572872 | tf_op jit(solution)/shard_map/ppermute | solution.py:22
  387.4 144.2 %collective-permute-start.18 = (f32[4,64,4,128]{3,2,1,0:T(4,128)}, f32[4,64,4,128]{3,2,1,0:T(4,128)}, u32[]{:S(2)}, u32[]{:S(2)}) collective-permute-start(f32[4,64,4,128]{3,2,1,0:T(4,128)} %get-tuple-element.15), channel_id=1, source_target_pairs={{0,16},{16,32},{32,48},{48,64},{64,80},{80,96},{96,112},{112,128},... | collective-permute-start | bytes 1572872 | tf_op jit(solution)/shard_map/ppermute | solution.py:19
  475.8 27.9 %copy-start.4 = (f32[4,64,8,128]{3,2,1,0:T(8,128)S(1)}, f32[4,64,8,128]{3,2,1,0:T(8,128)}, u32[]{:S(2)}) copy-start(f32[4,64,8,128]{3,2,1,0:T(8,128)} %copy-done.3) | copy-start | bytes 3145732
  531.5 3.8 copy-start.8
  531.5 3.8 copy-start.10
  531.5 3.8 copy-start.12
  531.5 3.8 copy-start.16
  543.9 28.2 %copy-start.18 = (f32[256,4]{1,0:T(8,128)S(1)}, f32[256,4]{1,0:T(8,128)}, u32[]{:S(2)}) copy-start(f32[256,4]{1,0:T(8,128)} %gather_fusion.1) | copy-start | bytes 12292
  543.9 28.2 %copy-start.19 = (f32[256,4]{1,0:T(8,128)S(1)}, f32[256,4]{1,0:T(8,128)}, u32[]{:S(2)}) copy-start(f32[256,4]{1,0:T(8,128)} %gather_fusion.2) | copy-start | bytes 12292
  543.9 202.3 %copy-start.1 = (bf16[4,32,32,128]{3,2,1,0:T(8,128)(2,1)S(1)}, bf16[4,32,32,128]{3,2,1,0:T(8,128)(2,1)}, u32[]{:S(2)}) copy-start(bf16[4,32,32,128]{3,2,1,0:T(8,128)(2,1)} %param.22) | copy-start | bytes 3145732
where the time goes:
time: 748 us; the launch traced here: 746 us
  blocking collectives  355 us (47%)
  starting transfers between devices  126 us (17%)
  local copies, waits for them, and re-layouts  122 us (16%)
  waiting for transfers between devices  84.8 us (11%)
  other arithmetic  52.8 us (7%)
    all_gather x4, blocking collectives, local(): acceleration = lax.all_gather(local_accel, 'dir', axis=0, tiled=True)  181 us
    psum x1, blocking collectives, local(): traces = lax.psum(jnp.stack(records, axis=1), 'tile')  174 us
    ppermute x12, waiting for transfers between devices, padded_2(): lax.ppermute(lax.slice_in_dim(block, 0, width, axis=dim), axis, backward)  67.6 us
    add x4, local copies, waits for them, and re-layouts, local(): 2.0 * current_born - earlier_born  64.7 us
    ppermute x12, starting transfers between devices, padded_2(): lax.ppermute(lax.slice_in_dim(block, block.shape[dim] - width, None, axis...  54.4 us
    ppermute x12, starting transfers between devices, padded_2(): lax.ppermute(lax.slice_in_dim(block, 0, width, axis=dim), axis, backward)  48.9 us
    gather x4, local copies, waits for them, and re-layouts, local(): jnp.take(following.reshape(following.shape[0], -1), flat_index, axis=1)  46.3 us
    add x4, other arithmetic, local(): 2.0 * current_born - earlier_born  28.4 us
  transfers between devices with their start and end apart: 26, of which 4 were waited for; matrix products, arithmetic and copies ran while one was open for 17% of the time, Pallas kernels for 0%

commit v1 on v0

--- a/solution.py
+++ b/solution.py
@@ -150,7 +150,7 @@
             * inside[None, :]
         )
         earlier_born, current_born = (current_born, following)
-    traces = lax.psum(jnp.stack(records, axis=1), "tile")
+    traces = jnp.sum(lax.all_gather(jnp.stack(records, axis=1), "tile"), axis=0)
     return (current_born, traces)
 
 

time: 748 us -> 638 us (0.85)
  blocking collectives: 355 us -> 238 us
    psum x1 -> x0, blocking collectives: 174 us -> none  [local(): traces = lax.psum(jnp.stack(records, axis=1), 'tile')]
    all_gather x0 -> x1, blocking collectives: none -> 57.3 us  [local(): traces = jnp.sum(lax.all_gather(jnp.stack(records, axis=1), 'tile'), axis=0)]
  transfers between devices with their start and end apart: 26 -> 26, of which waited for: 4 -> 4; matrix products, arithmetic and copies ran while one was open for 17% -> 20% of each run, Pallas kernels for 0% -> 0%
where the time goes in v1:
time: 638 us; the launch traced here: 631 us
  blocking collectives  238 us (37%)
  starting transfers between devices  126 us (20%)
  local copies, waits for them, and re-layouts  122 us (19%)
  waiting for transfers between devices  84.8 us (13%)
  other arithmetic  53.5 us (8%)
    all_gather x4, blocking collectives, local(): acceleration = lax.all_gather(local_accel, 'dir', axis=0, tiled=True)  181 us
    ppermute x12, waiting for transfers between devices, padded_2(): lax.ppermute(lax.slice_in_dim(block, 0, width, axis=dim), axis, backward)  67.6 us
    add x4, local copies, waits for them, and re-layouts, local(): 2.0 * current_born - earlier_born  64.7 us
    all_gather x1, blocking collectives, local(): traces = jnp.sum(lax.all_gather(jnp.stack(records, axis=1), 'tile'), axis=0)  57.3 us
    ppermute x12, starting transfers between devices, padded_2(): lax.ppermute(lax.slice_in_dim(block, block.shape[dim] - width, None, axis...  54.4 us
    ppermute x12, starting transfers between devices, padded_2(): lax.ppermute(lax.slice_in_dim(block, 0, width, axis=dim), axis, backward)  48.9 us
    gather x4, local copies, waits for them, and re-layouts, local(): jnp.take(following.reshape(following.shape[0], -1), flat_index, axis=1)  46.3 us
    add x4, other arithmetic, local(): 2.0 * current_born - earlier_born  28.4 us
  transfers between devices with their start and end apart: 26, of which 4 were waited for; matrix products, arithmetic and copies ran while one was open for 20% of the time, Pallas kernels for 0%

profile of v1, /device:TPU:24, one launch (start us, length us, event | category | flops | bytes accessed | tf_op | source)
XLA Modules:
  0.0 630.6 jit_solution(17042218702430523955)
XLA Ops:
  0.6 0.9 convert_reduce_fusion.1
  2.2 0.8 fusion.9
  3.8 17.9 %all-to-all-start = ((bf16[1,32,2]{2,0,1:T(2,128)(2,1)}), bf16[1,32,2]{2,0,1:T(2,128)(2,1)S(1)}, u32[]{:S(2)}, u32[]{:S(2)}) async-start(bf16[1,32,2]{2,0,1:T(2,128)(2,1)} %all_to_all.12), calls=%async_computation | async-start | bytes 32768 | tf_op jit(solution)/shard_map/all_to_all | solution.py:74
  21.8 0.8 convert_bitcast_fusion
  22.6 2.8 copy.41
  25.4 10.8 %all-to-all-done = bf16[1,32,2]{2,0,1:T(2,128)(2,1)S(1)} async-done(((bf16[1,32,2]{2,0,1:T(2,128)(2,1)}), bf16[1,32,2]{2,0,1:T(2,128)(2,1)S(1)}, u32[]{:S(2)}, u32[]{:S(2)}) %all-to-all-start) | async-done | bytes 160 | tf_op jit(solution)/shard_map/all_to_all | solution.py:74
  36.3 4.8 all-to-all-start.1
  41.8 4.0 collective-permute-start.3
  45.8 1.9 collective-permute-start.2
  47.7 1.1 fusion.119
  48.8 1.3 collective-permute-start.1
  50.1 3.8 collective-permute-start
  54.1 0.7 fusion.125
  56.8 0.9 slice_bitcast_fusion.2
  57.7 67.6 %collective-permute-done.3 = f32[1,4,8,128]{3,2,1,0:T(8,128)S(1)} collective-permute-done((f32[1,4,8,128]{3,2,1,0:T(8,128)S(1)}, f32[1,4,8,128]{3,2,1,0:T(8,128)S(1)}, u32[]{:S(2)}, u32[]{:S(2)}) %collective-permute-start.3) | collective-permute-done | bytes 16416 | tf_op jit(solution)/shard_map/ppermute | solution.py:22
  125.4 1.3 collective-permute-start.5
  126.7 3.0 collective-permute-start.4
  130.6 1.5 fusion.39
  132.1 27.6 %collective-permute-start.9 = (f32[1,4,8,128]{3,2,1,0:T(8,128)S(1)}, f32[1,4,8,128]{3,2,1,0:T(8,128)S(1)}, u32[]{:S(2)}, u32[]{:S(2)}) collective-permute-start(f32[1,4,8,128]{3,2,1,0:T(8,128)S(1)} %bitcast.138), channel_id=1, source_target_pairs={{1,0},{2,1},{3,2},{4,3},{5,4},{6,5},{7,6},{8,7},{9,8},{10,9},{11,1... | collective-permute-start | bytes 49160 | tf_op jit(solution)/shard_map/ppermute | solution.py:22
  159.8 1.9 collective-permute-start.8
  161.9 6.2 collective-permute-done.8
  168.1 1.3 collective-permute-start.11
  169.4 10.4 %collective-permute-start.10 = (f32[1,12,4,128]{3,2,1,0:T(4,128)S(1)}, f32[1,12,4,128]{3,2,1,0:T(4,128)S(1)}, u32[]{:S(2)}, u32[]{:S(2)}) collective-permute-start(f32[1,12,4,128]{3,2,1,0:T(4,128)S(1)} %get-tuple-element.26), channel_id=1, source_target_pairs={{0,16},{16,32},{32,48},{48,64},{64,80},{80,96},{96,112},{112,128},... | collective-permute-start | bytes 73736 | tf_op jit(solution)/shard_map/ppermute | solution.py:19
  179.8 37.0 %all_gather.18 = f32[64,8,128]{2,1,0:T(8,128)} all-gather(f32[4,8,128]{2,1,0:T(8,128)S(1)} %get-tuple-element.10), channel_id=1, replica_groups=mesh['tile'=32,'dir'=16] {'dir'}, dimensions={0}, use_global_device_ids=true | all-gather | bytes 278528 | tf_op jit(solution)/shard_map/all_gather | solution.py:136
  216.8 1.5 fusion.108
  218.3 3.6 collective-permute-start.15
  221.9 2.2 collective-permute-start.14
  224.2 5.3 select_maximum_fusion.6
  229.5 3.0 fusion.6
  232.5 7.7 %multiply_add_fusion.3 = f32[4,64,8,128]{3,2,1,0:T(8,128)S(1)} fusion(f32[4,64,8,128]{3,2,1,0:T(8,128)S(1)} %bitcast.133, f32[4,72,16,136]{3,2,1,0:T(8,128)S(1)} %copy-done.2, f32[4,64,4,128]{3,2,1,0:T(4,128)S(1)} %copy-done.15, f32[4,64,8,128]{3,2,1,0:T(8,128)S(1)} %convert_element_type.62, f32[4,64,4,128]{3,2,1,0:T(4,128)} %collective-permute-done, ...), kind=kLoop, calls=%fused_computation.110 | loop fusion | flops 23855104 | bytes 22806528 | tf_op jit(solution)/shard_map/add | solution.py:143
  240.4 1.4 collective-permute-start.7
  241.9 3.1 collective-permute-start.6
  245.0 1.3 collective-permute-start.17
  246.3 7.5 %collective-permute-start.16 = (f32[1,12,4,128]{3,2,1,0:T(4,128)S(1)}, f32[1,12,4,128]{3,2,1,0:T(4,128)S(1)}, u32[]{:S(2)}, u32[]{:S(2)}) collective-permute-start(f32[1,12,4,128]{3,2,1,0:T(4,128)S(1)} %get-tuple-element.24), channel_id=1, source_target_pairs={{0,16},{16,32},{32,48},{48,64},{64,80},{80,96},{96,112},{112,128},... | collective-permute-start | bytes 73736 | tf_op jit(solution)/shard_map/ppermute | solution.py:19
  253.7 49.0 %all_gather.19 = f32[64,8,128]{2,1,0:T(8,128)S(1)} all-gather(f32[4,8,128]{2,1,0:T(8,128)S(1)} %get-tuple-element.8), channel_id=1, replica_groups=mesh['tile'=32,'dir'=16] {'dir'}, dimensions={0}, use_global_device_ids=true | all-gather | bytes 278528 | tf_op jit(solution)/shard_map/all_gather | solution.py:136
  302.8 2.7 select_maximum_fusion.4
  305.5 6.1 multiply_add_fusion.2
  311.8 1.3 collective-permute-start.13
  313.1 3.1 collective-permute-start.12
  316.1 2.2 fusion.42
  318.4 3.2 collective-permute-start.21
  321.5 3.0 collective-permute-start.20
  324.5 46.2 %all_gather.20 = f32[64,8,128]{2,1,0:T(8,128)S(1)} all-gather(f32[4,8,128]{2,1,0:T(8,128)S(1)} %get-tuple-element.6), channel_id=1, replica_groups=mesh['tile'=32,'dir'=16] {'dir'}, dimensions={0}, use_global_device_ids=true | all-gather | bytes 278528 | tf_op jit(solution)/shard_map/all_gather | solution.py:136
  370.7 1.3 collective-permute-start.23
  372.0 3.2 collective-permute-start.22
  375.2 2.7 select_maximum_fusion.2
  377.9 6.1 multiply_add_fusion.1
  384.0 1.0 copy-done.3
  384.9 1.1 fusion.116
  386.1 1.3 collective-permute-start.19
  387.4 11.4 %collective-permute-start.18 = (f32[4,64,4,128]{3,2,1,0:T(4,128)}, f32[4,64,4,128]{3,2,1,0:T(4,128)}, u32[]{:S(2)}, u32[]{:S(2)}) collective-permute-start(f32[4,64,4,128]{3,2,1,0:T(4,128)} %get-tuple-element.11), channel_id=1, source_target_pairs={{0,16},{16,32},{32,48},{48,64},{64,80},{80,96},{96,112},{112,128},... | collective-permute-start | bytes 1572872 | tf_op jit(solution)/shard_map/ppermute | solution.py:19
  398.9 0.9 fusion.56
  399.7 48.9 %all_gather.21 = f32[64,8,128]{2,1,0:T(8,128)} all-gather(f32[4,8,128]{2,1,0:T(8,128)S(1)} %fusion.56), channel_id=1, replica_groups=mesh['tile'=32,'dir'=16] {'dir'}, dimensions={0}, use_global_device_ids=true | all-gather | bytes 278528 | tf_op jit(solution)/shard_map/all_gather | solution.py:136
  448.6 15.9 %copy.44 = f32[4,64,8,128]{0,3,2,1:T(8,128)} copy(f32[4,64,8,128]{3,2,1,0:T(8,128)S(1)} %multiply_add_fusion.3) | data formatting | bytes 2097152 | tf_op jit(solution)/shard_map/add | solution.py:143
  464.6 11.3 %gather_fusion = f32[256,4]{1,0:T(8,128)S(1)} fusion(f32[4,65536]{0,1:T(8,128)} %bitcast.129, s32[1024]{0:T(1024)S(1)} %pad_clamp_fusion), kind=kCustom, calls=%fused_computation.clone | custom fusion | bytes 9216 | tf_op jit(solution)/shard_map/jit(_take)/gather | solution.py:149
  475.8 16.0 %copy.45 = f32[4,64,8,128]{0,3,2,1:T(8,128)} copy(f32[4,64,8,128]{3,2,1,0:T(8,128)S(1)} %multiply_add_fusion.2) | data formatting | bytes 2097152 | tf_op jit(solution)/shard_map/add | solution.py:143
  491.8 11.9 %gather_fusion.1 = f32[256,4]{1,0:T(8,128)} fusion(f32[4,65536]{0,1:T(8,128)} %bitcast.131, s32[1024]{0:T(1024)S(1)} %pad_clamp_fusion), kind=kCustom, calls=%fused_computation.1.clone | custom fusion | bytes 9216 | tf_op jit(solution)/shard_map/jit(_take)/gather | solution.py:149
  503.7 16.0 %copy.46 = f32[4,64,8,128]{0,3,2,1:T(8,128)} copy(f32[4,64,8,128]{3,2,1,0:T(8,128)S(1)} %copy-done.4) | data formatting | bytes 2097152 | tf_op jit(solution)/shard_map/add | solution.py:143
  519.7 11.9 %gather_fusion.2 = f32[256,4]{1,0:T(8,128)} fusion(f32[4,65536]{0,1:T(8,128)} %bitcast.132, s32[1024]{0:T(1024)S(1)} %pad_clamp_fusion), kind=kCustom, calls=%fused_computation.2.clone | custom fusion | bytes 9216 | tf_op jit(solution)/shard_map/jit(_take)/gather | solution.py:149
  531.6 3.8 select_maximum_fusion
  535.4 8.5 %multiply_add_fusion = f32[4,64,8,128]{3,2,1,0:T(8,128)} fusion(f32[4,64,8,128]{3,2,1,0:T(8,128)S(1)} %bitcast.136, f32[4,72,16,136]{3,2,1,0:T(8,128)S(1)} %select_maximum_fusion, f32[4,64,4,128]{3,2,1,0:T(4,128)} %collective-permute-done.19, f32[4,64,8,128]{3,2,1,0:T(8,128)S(1)} %copy-done.4, f32[4,64,4,128]{3,2,1,0:T(4,128)} %collective-permute-done.18, ...), kind=kLoop, calls=%fused_computation.107 | loop fusion | flops 23592960 | bytes 23330816 | tf_op jit(solution)/shard_map/add | solution.py:143
  543.9 16.9 %copy.47 = f32[4,64,8,128]{0,3,2,1:T(8,128)} copy(f32[4,64,8,128]{3,2,1,0:T(8,128)} %multiply_add_fusion) | data formatting | bytes 2097152 | tf_op jit(solution)/shard_map/add | solution.py:143
  560.8 11.3 %gather_fusion.3 = f32[256,4]{1,0:T(8,128)S(1)} fusion(f32[4,65536]{0,1:T(8,128)} %bitcast.130, s32[1024]{0:T(1024)S(1)} %pad_clamp_fusion), kind=kCustom, calls=%fused_computation.3.clone | custom fusion | bytes 9216 | tf_op jit(solution)/shard_map/jit(_take)/gather | solution.py:149
  572.6 57.3 %all-gather = f32[128,4,256]{2,1,0:T(4,128)S(1)} all-gather(f32[4,4,256]{2,1,0:T(4,128)S(1)} %pad_maximum_fusion.12), channel_id=2, replica_groups=mesh['tile'=32,'dir'=16] {'tile'}, dimensions={0}, use_global_device_ids=true | all-gather | bytes 540672 | tf_op jit(solution)/shard_map/all_gather | solution.py:153
  (112 shorter events, 7.0 us)
Async XLA Ops:
  0.6 21.2 %copy-start = (bf16[4,32,32,128]{3,2,1,0:T(8,128)(2,1)S(1)}, bf16[4,32,32,128]{3,2,1,0:T(8,128)(2,1)}, u32[]{:S(2)}) copy-start(bf16[4,32,32,128]{3,2,1,0:T(8,128)(2,1)} %param.22) | copy-start | bytes 3145732
  3.8 32.4 %all-to-all-start = ((bf16[1,32,2]{2,0,1:T(2,128)(2,1)}), bf16[1,32,2]{2,0,1:T(2,128)(2,1)S(1)}, u32[]{:S(2)}, u32[]{:S(2)}) async-start(bf16[1,32,2]{2,0,1:T(2,128)(2,1)} %all_to_all.12), calls=%async_computation | async-start | bytes 32768 | tf_op jit(solution)/shard_map/all_to_all | solution.py:74
  22.6 25.1 %copy-start.5 = (bf16[4,64,8,128]{3,2,1,0:T(8,128)(2,1)S(1)}, bf16[4,64,8,128]{3,2,1,0:T(8,128)(2,1)}, u32[]{:S(2)}) copy-start(bf16[4,64,8,128]{3,2,1,0:T(8,128)(2,1)} %param.21) | copy-start | bytes 1572868
  22.6 31.3 %copy-start.17 = (bf16[3,64,8,128]{3,2,1,0:T(8,128)(2,1)S(1)}, bf16[3,64,8,128]{3,2,1,0:T(8,128)(2,1)}, u32[]{:S(2)}) copy-start(bf16[3,64,8,128]{3,2,1,0:T(8,128)(2,1)} %param.19) | copy-start | bytes 1179652
  25.4 28.6 %copy-start.21 = (s32[3]{0:T(128)S(1)}, s32[3]{0:T(128)}, u32[]{:S(2)}) copy-start(s32[3]{0:T(128)} %param.26) | copy-start | bytes 40
  25.4 30.6 %copy-start.22 = (f32[4]{0:T(128)S(1)}, f32[4]{0:T(128)}, u32[]{:S(2)}) copy-start(f32[4]{0:T(128)} %param.25) | copy-start | bytes 52
  25.4 31.4 %copy-start.23 = (s32[256]{0:T(256)S(1)}, s32[256]{0:T(256)}, u32[]{:S(2)}) copy-start(s32[256]{0:T(256)} %param.29) | copy-start | bytes 3076
  25.4 31.4 %copy-start.24 = (s32[256]{0:T(256)S(1)}, s32[256]{0:T(256)}, u32[]{:S(2)}) copy-start(s32[256]{0:T(256)} %param.28) | copy-start | bytes 3076
  25.4 31.4 %copy-start.25 = (s32[256]{0:T(256)S(1)}, s32[256]{0:T(256)}, u32[]{:S(2)}) copy-start(s32[256]{0:T(256)} %param.27) | copy-start | bytes 3076
  25.4 105.0 %copy-start.20 = (bf16[64,8,128]{2,1,0:T(8,128)(2,1)S(1)}, bf16[64,8,128]{2,1,0:T(8,128)(2,1)}, u32[]{:S(2)}) copy-start(bf16[64,8,128]{2,1,0:T(8,128)(2,1)} %param.18) | copy-start | bytes 393220
  36.3 193.2 %all-to-all-start.1 = ((bf16[4,64,32,128]{3,2,0,1:T(8,128)(2,1)}), bf16[4,64,32,128]{3,2,0,1:T(8,128)(2,1)}, u32[]{:S(2)}, u32[]{:S(2)}) async-start(bf16[4,64,32,128]{3,2,0,1:T(8,128)(2,1)} %copy.41), calls=%async_computation.1 | async-start | bytes 4194304 | tf_op jit(solution)/shard_map/all_to_all | solution.py:73
  41.8 83.6 %collective-permute-start.3 = (f32[1,4,8,128]{3,2,1,0:T(8,128)S(1)}, f32[1,4,8,128]{3,2,1,0:T(8,128)S(1)}, u32[]{:S(2)}, u32[]{:S(2)}) collective-permute-start(f32[1,4,8,128]{3,2,1,0:T(8,128)S(1)} %dynamic-slice_bitcast_fusion.3), channel_id=1, source_target_pairs={{1,0},{2,1},{3,2},{4,3},{5,4},{6,5},{7,6},{8,7},{9,8},{10,9},{11,1... | collective-permute-start | bytes 49160 | tf_op jit(solution)/shard_map/ppermute | solution.py:22
  45.8 79.6 %collective-permute-start.2 = (f32[1,4,8,128]{3,2,1,0:T(8,128)S(1)}, f32[1,4,8,128]{3,2,1,0:T(8,128)S(1)}, u32[]{:S(2)}, u32[]{:S(2)}) collective-permute-start(f32[1,4,8,128]{3,2,1,0:T(8,128)S(1)} %dynamic-slice_bitcast_fusion.3), channel_id=1, source_target_pairs={{0,1},{1,2},{2,3},{3,4},{4,5},{5,6},{6,7},{7,8},{8,9},{9,10},{10,1... | collective-permute-start | bytes 49160 | tf_op jit(solution)/shard_map/ppermute | solution.py:19
  48.8 175.3 %collective-permute-start.1 = (f32[4,64,4,128]{3,2,1,0:T(4,128)}, f32[4,64,4,128]{3,2,1,0:T(4,128)S(1)}, u32[]{:S(2)}, u32[]{:S(2)}) collective-permute-start(f32[4,64,4,128]{3,2,1,0:T(4,128)} %get-tuple-element.21), channel_id=1, source_target_pairs={{16,0},{32,16},{48,32},{64,48},{80,64},{96,80},{112,96},{128,112},... | collective-permute-start | bytes 1572872 | tf_op jit(solution)/shard_map/ppermute | solution.py:22
  50.1 174.0 %collective-permute-start = (f32[4,64,4,128]{3,2,1,0:T(4,128)}, f32[4,64,4,128]{3,2,1,0:T(4,128)}, u32[]{:S(2)}, u32[]{:S(2)}) collective-permute-start(f32[4,64,4,128]{3,2,1,0:T(4,128)} %get-tuple-element.20), channel_id=1, source_target_pairs={{0,16},{16,32},{32,48},{48,64},{64,80},{80,96},{96,112},{112,128},... | collective-permute-start | bytes 1572872 | tf_op jit(solution)/shard_map/ppermute | solution.py:19
  54.0 175.4 %copy-start.13 = (f32[3,64,8,128]{3,2,1,0:T(8,128)}, f32[3,64,8,128]{3,2,1,0:T(8,128)S(1)}, u32[]{:S(2)}) copy-start(f32[3,64,8,128]{3,2,1,0:T(8,128)S(1)} %convert_element_type.65) | copy-start | bytes 2359300
  125.4 5.1 collective-permute-start.5
  126.7 3.9 collective-permute-start.4
  132.1 29.7 %collective-permute-start.9 = (f32[1,4,8,128]{3,2,1,0:T(8,128)S(1)}, f32[1,4,8,128]{3,2,1,0:T(8,128)S(1)}, u32[]{:S(2)}, u32[]{:S(2)}) collective-permute-start(f32[1,4,8,128]{3,2,1,0:T(8,128)S(1)} %bitcast.138), channel_id=1, source_target_pairs={{1,0},{2,1},{3,2},{4,3},{5,4},{6,5},{7,6},{8,7},{9,8},{10,9},{11,1... | collective-permute-start | bytes 49160 | tf_op jit(solution)/shard_map/ppermute | solution.py:22
  159.8 8.3 %collective-permute-start.8 = (f32[1,4,8,128]{3,2,1,0:T(8,128)S(1)}, f32[1,4,8,128]{3,2,1,0:T(8,128)S(1)}, u32[]{:S(2)}, u32[]{:S(2)}) collective-permute-start(f32[1,4,8,128]{3,2,1,0:T(8,128)S(1)} %bitcast.139), channel_id=1, source_target_pairs={{0,1},{1,2},{2,3},{3,4},{4,5},{5,6},{6,7},{7,8},{8,9},{9,10},{10,1... | collective-permute-start | bytes 49160 | tf_op jit(solution)/shard_map/ppermute | solution.py:19
  168.1 48.6 %collective-permute-start.11 = (f32[1,12,4,128]{3,2,1,0:T(4,128)S(1)}, f32[1,12,4,128]{3,2,1,0:T(4,128)S(1)}, u32[]{:S(2)}, u32[]{:S(2)}) collective-permute-start(f32[1,12,4,128]{3,2,1,0:T(4,128)S(1)} %get-tuple-element.27), channel_id=1, source_target_pairs={{16,0},{32,16},{48,32},{64,48},{80,64},{96,80},{112,96},{128,112},... | collective-permute-start | bytes 73736 | tf_op jit(solution)/shard_map/ppermute | solution.py:22
  169.4 47.3 %collective-permute-start.10 = (f32[1,12,4,128]{3,2,1,0:T(4,128)S(1)}, f32[1,12,4,128]{3,2,1,0:T(4,128)S(1)}, u32[]{:S(2)}, u32[]{:S(2)}) collective-permute-start(f32[1,12,4,128]{3,2,1,0:T(4,128)S(1)} %get-tuple-element.26), channel_id=1, source_target_pairs={{0,16},{16,32},{32,48},{48,64},{64,80},{80,96},{96,112},{112,128},... | collective-permute-start | bytes 73736 | tf_op jit(solution)/shard_map/ppermute | solution.py:19
  218.3 26.6 %collective-permute-start.15 = (f32[1,4,8,128]{3,2,1,0:T(8,128)S(1)}, f32[1,4,8,128]{3,2,1,0:T(8,128)S(1)}, u32[]{:S(2)}, u32[]{:S(2)}) collective-permute-start(f32[1,4,8,128]{3,2,1,0:T(8,128)S(1)} %get-tuple-element.7), channel_id=1, source_target_pairs={{1,0},{2,1},{3,2},{4,3},{5,4},{6,5},{7,6},{8,7},{9,8},{10,9},{11,1... | collective-permute-start | bytes 49160 | tf_op jit(solution)/shard_map/ppermute | solution.py:22
  221.9 23.0 %collective-permute-start.14 = (f32[1,4,8,128]{3,2,1,0:T(8,128)S(1)}, f32[1,4,8,128]{3,2,1,0:T(8,128)S(1)}, u32[]{:S(2)}, u32[]{:S(2)}) collective-permute-start(f32[1,4,8,128]{3,2,1,0:T(8,128)S(1)} %get-tuple-element.7), channel_id=1, source_target_pairs={{0,1},{1,2},{2,3},{3,4},{4,5},{5,6},{6,7},{7,8},{8,9},{9,10},{10,1... | collective-permute-start | bytes 49160 | tf_op jit(solution)/shard_map/ppermute | solution.py:19
  224.2 5.3 copy-start.14
  229.5 3.1 copy-start.2
  229.5 3.1 copy-start.15
  240.2 65.2 %copy-start.6 = (bf16[4,64,8,128]{3,2,1,0:T(8,128)(2,1)S(1)}, bf16[4,64,8,128]{3,2,1,0:T(8,128)(2,1)}, u32[]{:S(2)}) copy-start(bf16[4,64,8,128]{3,2,1,0:T(8,128)(2,1)} %param.21) | copy-start | bytes 1572868
  240.2 65.2 %copy-start.7 = (f32[64,8,128]{2,1,0:T(8,128)S(1)}, f32[64,8,128]{2,1,0:T(8,128)}, u32[]{:S(2)}) copy-start(f32[64,8,128]{2,1,0:T(8,128)} %get-tuple-element.17) | copy-start | bytes 786436
  240.2 65.2 %copy-start.9 = (f32[64,8,128]{2,1,0:T(8,128)S(1)}, f32[64,8,128]{2,1,0:T(8,128)}, u32[]{:S(2)}) copy-start(f32[64,8,128]{2,1,0:T(8,128)} %get-tuple-element.18) | copy-start | bytes 786436
  240.2 65.2 %copy-start.11 = (f32[64,8,128]{2,1,0:T(8,128)S(1)}, f32[64,8,128]{2,1,0:T(8,128)}, u32[]{:S(2)}) copy-start(f32[64,8,128]{2,1,0:T(8,128)} %get-tuple-element.19) | copy-start | bytes 786436
  240.4 62.3 %collective-permute-start.7 = (f32[4,64,4,128]{3,2,1,0:T(4,128)S(1)}, f32[4,64,4,128]{3,2,1,0:T(4,128)S(1)}, u32[]{:S(2)}, u32[]{:S(2)}) collective-permute-start(f32[4,64,4,128]{3,2,1,0:T(4,128)S(1)} %get-tuple-element.16), channel_id=1, source_target_pairs={{16,0},{32,16},{48,32},{64,48},{80,64},{96,80},{112,96},{128,112},... | collective-permute-start | bytes 1572872 | tf_op jit(solution)/shard_map/ppermute | solution.py:22
  241.9 60.9 %collective-permute-start.6 = (f32[4,64,4,128]{3,2,1,0:T(4,128)S(1)}, f32[4,64,4,128]{3,2,1,0:T(4,128)S(1)}, u32[]{:S(2)}, u32[]{:S(2)}) collective-permute-start(f32[4,64,4,128]{3,2,1,0:T(4,128)S(1)} %get-tuple-element.15), channel_id=1, source_target_pairs={{0,16},{16,32},{32,48},{48,64},{64,80},{80,96},{96,112},{112,128},... | collective-permute-start | bytes 1572872 | tf_op jit(solution)/shard_map/ppermute | solution.py:19
  245.0 57.7 %collective-permute-start.17 = (f32[1,12,4,128]{3,2,1,0:T(4,128)S(1)}, f32[1,12,4,128]{3,2,1,0:T(4,128)S(1)}, u32[]{:S(2)}, u32[]{:S(2)}) collective-permute-start(f32[1,12,4,128]{3,2,1,0:T(4,128)S(1)} %get-tuple-element.25), channel_id=1, source_target_pairs={{16,0},{32,16},{48,32},{64,48},{80,64},{96,80},{112,96},{128,112},... | collective-permute-start | bytes 73736 | tf_op jit(solution)/shard_map/ppermute | solution.py:22
  246.3 56.4 %collective-permute-start.16 = (f32[1,12,4,128]{3,2,1,0:T(4,128)S(1)}, f32[1,12,4,128]{3,2,1,0:T(4,128)S(1)}, u32[]{:S(2)}, u32[]{:S(2)}) collective-permute-start(f32[1,12,4,128]{3,2,1,0:T(4,128)S(1)} %get-tuple-element.24), channel_id=1, source_target_pairs={{0,16},{16,32},{32,48},{48,64},{64,80},{80,96},{96,112},{112,128},... | collective-permute-start | bytes 73736 | tf_op jit(solution)/shard_map/ppermute | solution.py:19
  311.8 63.4 %collective-permute-start.13 = (f32[4,64,4,128]{3,2,1,0:T(4,128)S(1)}, f32[4,64,4,128]{3,2,1,0:T(4,128)S(1)}, u32[]{:S(2)}, u32[]{:S(2)}) collective-permute-start(f32[4,64,4,128]{3,2,1,0:T(4,128)S(1)} %get-tuple-element.14), channel_id=1, source_target_pairs={{16,0},{32,16},{48,32},{64,48},{80,64},{96,80},{112,96},{128,112},... | collective-permute-start | bytes 1572872 | tf_op jit(solution)/shard_map/ppermute | solution.py:22
  313.1 62.1 %collective-permute-start.12 = (f32[4,64,4,128]{3,2,1,0:T(4,128)S(1)}, f32[4,64,4,128]{3,2,1,0:T(4,128)S(1)}, u32[]{:S(2)}, u32[]{:S(2)}) collective-permute-start(f32[4,64,4,128]{3,2,1,0:T(4,128)S(1)} %get-tuple-element.13), channel_id=1, source_target_pairs={{0,16},{16,32},{32,48},{48,64},{64,80},{80,96},{96,112},{112,128},... | collective-permute-start | bytes 1572872 | tf_op jit(solution)/shard_map/ppermute | solution.py:19
  318.4 52.3 %collective-permute-start.21 = (f32[1,4,8,128]{3,2,1,0:T(8,128)S(1)}, f32[1,4,8,128]{3,2,1,0:T(8,128)S(1)}, u32[]{:S(2)}, u32[]{:S(2)}) collective-permute-start(f32[1,4,8,128]{3,2,1,0:T(8,128)S(1)} %get-tuple-element.5), channel_id=1, source_target_pairs={{1,0},{2,1},{3,2},{4,3},{5,4},{6,5},{7,6},{8,7},{9,8},{10,9},{11,1... | collective-permute-start | bytes 49160 | tf_op jit(solution)/shard_map/ppermute | solution.py:22
  321.5 49.1 %collective-permute-start.20 = (f32[1,4,8,128]{3,2,1,0:T(8,128)S(1)}, f32[1,4,8,128]{3,2,1,0:T(8,128)S(1)}, u32[]{:S(2)}, u32[]{:S(2)}) collective-permute-start(f32[1,4,8,128]{3,2,1,0:T(8,128)S(1)} %get-tuple-element.5), channel_id=1, source_target_pairs={{0,1},{1,2},{2,3},{3,4},{4,5},{5,6},{6,7},{7,8},{8,9},{9,10},{10,1... | collective-permute-start | bytes 49160 | tf_op jit(solution)/shard_map/ppermute | solution.py:19
  370.7 28.1 %collective-permute-start.23 = (f32[1,12,4,128]{3,2,1,0:T(4,128)S(1)}, f32[1,12,4,128]{3,2,1,0:T(4,128)S(1)}, u32[]{:S(2)}, u32[]{:S(2)}) collective-permute-start(f32[1,12,4,128]{3,2,1,0:T(4,128)S(1)} %get-tuple-element.23), channel_id=1, source_target_pairs={{16,0},{32,16},{48,32},{64,48},{80,64},{96,80},{112,96},{128,112},... | collective-permute-start | bytes 73736 | tf_op jit(solution)/shard_map/ppermute | solution.py:22
  372.0 26.8 %collective-permute-start.22 = (f32[1,12,4,128]{3,2,1,0:T(4,128)S(1)}, f32[1,12,4,128]{3,2,1,0:T(4,128)S(1)}, u32[]{:S(2)}, u32[]{:S(2)}) collective-permute-start(f32[1,12,4,128]{3,2,1,0:T(4,128)S(1)} %get-tuple-element.22), channel_id=1, source_target_pairs={{0,16},{16,32},{32,48},{48,64},{64,80},{80,96},{96,112},{112,128},... | collective-permute-start | bytes 73736 | tf_op jit(solution)/shard_map/ppermute | solution.py:19
  384.0 1.0 copy-start.3
  386.1 145.5 %collective-permute-start.19 = (f32[4,64,4,128]{3,2,1,0:T(4,128)}, f32[4,64,4,128]{3,2,1,0:T(4,128)}, u32[]{:S(2)}, u32[]{:S(2)}) collective-permute-start(f32[4,64,4,128]{3,2,1,0:T(4,128)} %get-tuple-element.12), channel_id=1, source_target_pairs={{16,0},{32,16},{48,32},{64,48},{80,64},{96,80},{112,96},{128,112},... | collective-permute-start | bytes 1572872 | tf_op jit(solution)/shard_map/ppermute | solution.py:22
  387.4 144.2 %collective-permute-start.18 = (f32[4,64,4,128]{3,2,1,0:T(4,128)}, f32[4,64,4,128]{3,2,1,0:T(4,128)}, u32[]{:S(2)}, u32[]{:S(2)}) collective-permute-start(f32[4,64,4,128]{3,2,1,0:T(4,128)} %get-tuple-element.11), channel_id=1, source_target_pairs={{0,16},{16,32},{32,48},{48,64},{64,80},{80,96},{96,112},{112,128},... | collective-permute-start | bytes 1572872 | tf_op jit(solution)/shard_map/ppermute | solution.py:19
  475.8 27.9 %copy-start.4 = (f32[4,64,8,128]{3,2,1,0:T(8,128)S(1)}, f32[4,64,8,128]{3,2,1,0:T(8,128)}, u32[]{:S(2)}) copy-start(f32[4,64,8,128]{3,2,1,0:T(8,128)} %copy-done.3) | copy-start | bytes 3145732
  531.5 3.8 copy-start.8
  531.5 3.8 copy-start.10
  531.5 3.8 copy-start.12
  531.5 3.8 copy-start.16
  543.9 28.2 %copy-start.18 = (f32[256,4]{1,0:T(8,128)S(1)}, f32[256,4]{1,0:T(8,128)}, u32[]{:S(2)}) copy-start(f32[256,4]{1,0:T(8,128)} %gather_fusion.1) | copy-start | bytes 12292
  543.9 28.2 %copy-start.19 = (f32[256,4]{1,0:T(8,128)S(1)}, f32[256,4]{1,0:T(8,128)}, u32[]{:S(2)}) copy-start(f32[256,4]{1,0:T(8,128)} %gather_fusion.2) | copy-start | bytes 12292
  543.9 86.7 %copy-start.1 = (bf16[4,32,32,128]{3,2,1,0:T(8,128)(2,1)S(1)}, bf16[4,32,32,128]{3,2,1,0:T(8,128)(2,1)}, u32[]{:S(2)}) copy-start(bf16[4,32,32,128]{3,2,1,0:T(8,128)(2,1)} %param.22) | copy-start | bytes 3145732
